TPU v7x, 32 devices: a whole 2x2x4 slice. The times are simulated.
32 devices in a mesh: grp: 2 (over y), row: 8 (over z, x), sub: 2 (over core).
Axes of the slice: x: 2, y: 2, z: 4, core: 2. Of those that a mesh axis runs over, the one named last changes fastest.
Arguments:
- pair_rep: bfloat16 [64, 32, 128], P(('grp', 'row'), 'sub'), parts along dimension 0, may hold values from -6 to 6
- norm_gain: float32 [128], replicated, may hold values from 0.1 to 1.9
- norm_bias: float32 [128], replicated, may hold values from -3 to 3
- w_a_proj: bfloat16 [128, 128], replicated, may hold values from -0.5 to 0.5
- w_a_gate: bfloat16 [128, 128], replicated, may hold values from -0.5 to 0.5
- w_b_proj: bfloat16 [128, 128], replicated, may hold values from -0.5 to 0.5
- w_b_gate: bfloat16 [128, 128], replicated, may hold values from -0.5 to 0.5
- w_gate: bfloat16 [128, 128], replicated, may hold values from -0.5 to 0.5
- out_gain: float32 [128], replicated, may hold values from 0.1 to 1.9
- out_bias: float32 [128], replicated, may hold values from -3 to 3
- w_out: bfloat16 [128, 128], replicated, may hold values from -0.5 to 0.5
Outputs:
- update: bfloat16 [64, 32, 128], P(('grp', 'row'), 'sub'), parts along dimension 0
There are 2 independent parts, one for each index of `grp`. A program takes and returns all parts, laid end to end along the dimension named above; an argument that names none is the same for every part. Nothing has to cross between parts.
All inputs are finite; a program needn't handle non-finite values.
Results may differ from a plain program's by a relative error of at most 0.012.
Values may be sent and summed in bfloat16 or wider, within the bound.
A program may use at most 64 MiB of HBM per device.

v0:
```python
import functools

import jax
import jax.numpy as jnp
from jax import lax
from jax.experimental import pallas as pl
from jax.experimental.pallas import tpu as pltpu
from jax.sharding import PartitionSpec as P

EPSILON = 1e-05


def layer_norm(values, gain, shift, axis):
    centred = values - jnp.mean(values, axis=axis, keepdims=True)
    variance = jnp.mean(centred * centred, axis=axis, keepdims=True)
    return centred * lax.rsqrt(variance + EPSILON) * gain + shift


def per_device(
    pair_rep,
    norm_gain,
    norm_bias,
    w_a_proj,
    w_a_gate,
    w_b_proj,
    w_b_gate,
    w_gate,
    out_gain,
    out_bias,
    w_out,
):
    hidden = w_a_proj.shape[1]
    w_inner = jnp.concatenate([w_a_proj, w_a_gate, w_b_proj, w_b_gate], axis=1)
    normed = layer_norm(pair_rep.astype(jnp.float32), norm_gain, norm_bias, -1).astype(jnp.bfloat16)
    inner = jnp.einsum("rkc,cm->mrk", normed, w_inner, preferred_element_type=jnp.float32)
    left_local = (jax.nn.sigmoid(inner[hidden : 2 * hidden]) * inner[:hidden]).astype(jnp.bfloat16)
    right_local = (
        jax.nn.sigmoid(inner[3 * hidden : 4 * hidden]) * inner[2 * hidden : 3 * hidden]
    ).astype(jnp.bfloat16)
    gating = jax.nn.sigmoid(
        jnp.einsum("rkc,cd->rkd", normed, w_gate, preferred_element_type=jnp.float32)
    ).astype(jnp.bfloat16)
    left_chan, right_chan = (
        lax.all_to_all(left_local, "row", split_axis=0, concat_axis=1, tiled=True),
        lax.all_to_all(right_local, "row", split_axis=0, concat_axis=1, tiled=True),
    )
    left_rows = lax.all_to_all(left_chan, "sub", split_axis=1, concat_axis=2, tiled=True)
    triangle = jnp.einsum(
        "hik,hjk->hij",
        left_rows,
        lax.all_gather(right_chan, "sub", axis=2, tiled=True),
        preferred_element_type=jnp.float32,
    ).astype(jnp.bfloat16)
    regrouped = lax.all_to_all(
        lax.all_to_all(triangle, "sub", split_axis=2, concat_axis=1, tiled=True),
        "row",
        split_axis=1,
        concat_axis=0,
        tiled=True,
    )
    hidden_normed = layer_norm(
        regrouped.astype(jnp.float32), out_gain[:, None, None], out_bias[:, None, None], 0
    ).astype(jnp.bfloat16)
    mixed = jnp.einsum("hrj,hc->rjc", hidden_normed, w_out, preferred_element_type=jnp.float32)
    return (gating.astype(jnp.float32) * mixed).astype(jnp.bfloat16)


def gated(normed, weights):
    hidden = weights.shape[1] // 2
    inner = jnp.dot(normed, weights, preferred_element_type=jnp.float32)
    return (jax.nn.sigmoid(inner[:, hidden:]) * inner[:, :hidden]).astype(jnp.bfloat16)


def kernel(
    n_row,
    pair_hbm,
    ngain_hbm,
    nbias_hbm,
    wap_hbm,
    wag_hbm,
    wbp_hbm,
    wbg_hbm,
    wg_hbm,
    ogain_hbm,
    obias_hbm,
    wo_hbm,
    out_ref,
    pair_v,
    vec_v,
    w_v,
    wo_v,
    right_send,
    right_buf,
    left_buf,
    tri_v,
    in_sem,
    send_sem,
    recv_sem,
    left_sem,
    ready,
    late,
):
    rows, cols, chan = pair_v.shape
    hidden = right_send.shape[-1]
    half = n_row // 2
    row = lax.axis_index("row")
    sub = lax.axis_index("sub")
    other = 1 - sub
    owner = row // half
    slot = lax.rem(row, half)
    near = sub == owner
    low = owner == 0
    low_near = jnp.logical_and(low, sub == 0)
    low_far = jnp.logical_and(low, sub == 1)
    high_near = jnp.logical_and(owner == 1, sub == 1)
    high_far = jnp.logical_and(owner == 1, sub == 0)
    last = row == n_row - 1
    split = half // 2
    mid = jnp.logical_and(owner == 1, slot < split)
    outer = jnp.logical_and(owner == 1, jnp.logical_and(slot >= split, jnp.logical_not(last)))

    loads = [
        pltpu.make_async_copy(pair_hbm, pair_v, in_sem.at[0]),
        pltpu.make_async_copy(ngain_hbm, vec_v.at[0], in_sem.at[1]),
        pltpu.make_async_copy(nbias_hbm, vec_v.at[1], in_sem.at[2]),
        pltpu.make_async_copy(wbp_hbm, w_v.at[:, 0:hidden], in_sem.at[3]),
        pltpu.make_async_copy(wbg_hbm, w_v.at[:, hidden : 2 * hidden], in_sem.at[4]),
        pltpu.make_async_copy(wap_hbm, w_v.at[:, 2 * hidden : 3 * hidden], in_sem.at[5]),
        pltpu.make_async_copy(wag_hbm, w_v.at[:, 3 * hidden : 4 * hidden], in_sem.at[6]),
        pltpu.make_async_copy(wg_hbm, w_v.at[:, 4 * hidden : 4 * hidden + chan], in_sem.at[7]),
        pltpu.make_async_copy(ogain_hbm, vec_v.at[2], in_sem.at[8]),
        pltpu.make_async_copy(obias_hbm, vec_v.at[3], in_sem.at[9]),
        pltpu.make_async_copy(wo_hbm, wo_v, in_sem.at[10]),
    ]
    for load in loads:
        load.start()

    barrier = pltpu.get_barrier_semaphore()

    def greet(semaphore, target):
        pl.semaphore_signal(
            semaphore, inc=1, device_id=target, device_id_type=pl.DeviceIdType.MESH
        )

    @pl.when(low_near)
    def _():
        for step in range(1, half):
            greet(barrier, {"row": lax.rem(slot + step, half), "sub": 0})

    @pl.when(low_far)
    def _():
        greet(barrier, {"sub": 0})
        for step in range(half)[::-1]:
            greet(barrier, {"row": half + step, "sub": 0})
            if step >= split:
                greet(barrier, {"row": half + step, "sub": 1})

    @pl.when(jnp.logical_and(high_far, jnp.logical_not(last)))
    def _():
        for step in range(half):
            greet(barrier, {"row": step, "sub": 1})

    @pl.when(high_near)
    def _():
        greet(barrier, {"sub": 0})
        for step in range(half):

            @pl.when(slot != step)
            def _():
                greet(barrier, {"row": half + step, "sub": 1})
                if step >= split:
                    greet(barrier, {"row": half + step, "sub": 0})

    left_copy = pltpu.make_async_remote_copy(
        src_ref=left_buf.at[sub],
        dst_ref=left_buf.at[sub],
        send_sem=send_sem.at[n_row],
        recv_sem=left_sem,
        device_id={"sub": other},
        device_id_type=pl.DeviceIdType.MESH,
    )

    def block_copy(source, index, target_row, target_sub):
        return pltpu.make_async_remote_copy(
            src_ref=source,
            dst_ref=right_buf.at[slot, sub],
            send_sem=send_sem.at[index],
            recv_sem=recv_sem.at[slot, sub],
            device_id={"row": target_row, "sub": target_sub},
            device_id_type=pl.DeviceIdType.MESH,
        )

    raw_copy = block_copy(pair_hbm, 0, 0, owner)
    copies = [block_copy(right_send, q, q, owner) for q in range(n_row)]
    copies[half:] = [
        block_copy(right_send, q, q, jnp.where(low, 0, 1)) for q in range(half, n_row)
    ]
    sent = [jnp.logical_not(jnp.logical_and(near, row == q)) for q in range(n_row)]

    def start(first, end, guarded):
        for q in range(first, end):
            if guarded:

                @pl.when(sent[q])
                def _():
                    copies[q].start()
            else:
                copies[q].start()

    @pl.when(low_near)
    def _():
        pl.semaphore_wait(barrier, half)
        greet(ready, {"sub": 1})

    @pl.when(jnp.logical_and(high_far, mid))
    def _():
        pl.semaphore_wait(barrier, half + 1)
        greet(ready, {"sub": 1})

    @pl.when(last)
    def _():
        pl.semaphore_wait(barrier, 2 * half - sub)
        raw_copy.start()

        @pl.when(sub == 0)
        def _():
            greet(ready, {"sub": 1})
            for step in range(half):
                greet(late, {"row": step, "sub": 1})

    for load in loads[:3]:
        load.wait()
    pair = pair_v[...].astype(jnp.float32).reshape(rows * cols, chan)
    normed = layer_norm(pair, vec_v[0], vec_v[1], -1).astype(jnp.bfloat16)
    for load in loads[3:5]:
        load.wait()
    right = gated(normed, w_v[:, 0 : 2 * hidden]).reshape(rows, cols, hidden)
    right_send[...] = right

    @pl.when(low_far)
    def _():
        pl.semaphore_wait(ready, 1)

    @pl.when(jnp.logical_and(high_near, mid))
    def _():
        pl.semaphore_wait(ready, 1)

    @pl.when(outer)
    def _():
        pl.semaphore_wait(barrier, 2 * half - sub)

        @pl.when(sub == 0)
        def _():
            greet(ready, {"sub": 1})

    @pl.when(jnp.logical_and(sent[0], jnp.logical_not(last)))
    def _():
        copies[0].start()

    start(1, half, True)

    @pl.when(near)
    def _():
        right_buf[slot, sub] = right

    for load in loads[5:7]:
        load.wait()
    left = gated(normed, w_v[:, 2 * hidden : 4 * hidden])
    left_buf[sub] = left.reshape(rows, cols, hidden)

    @pl.when(jnp.logical_and(high_near, jnp.logical_not(mid)))
    def _():
        pl.semaphore_wait(ready, 1)

    left_copy.start()

    @pl.when(jnp.logical_and(high_near, mid))
    def _():
        pl.semaphore_wait(barrier, half - 1)
        greet(ready, {"sub": 0})

    @pl.when(jnp.logical_and(high_far, mid))
    def _():
        pl.semaphore_wait(ready, 1)

    @pl.when(jnp.logical_not(low))
    def _():
        start(half, n_row, True)

    loads[7].wait()
    gating = jax.nn.sigmoid(
        jnp.dot(
            normed, w_v[:, 4 * hidden : 4 * hidden + chan], preferred_element_type=jnp.float32
        )
    ).astype(jnp.bfloat16)
    for load in loads[8:]:
        load.wait()

    @pl.when(low_far)
    def _():
        pl.semaphore_wait(barrier, half - 1)
        greet(ready, {"sub": 0})

    @pl.when(low_near)
    def _():
        pl.semaphore_wait(ready, 1)

    @pl.when(low)
    def _():
        start(half, n_row - 1, False)
        pl.semaphore_wait(late, 1)

    @pl.when(low_far)
    def _():
        greet(late, {"sub": 0})

    @pl.when(low)
    def _():
        copies[-1].start()

    left_copy.wait_recv()
    left_all = left_buf[...].astype(jnp.float32)
    for source in range(half):
        for source_sub in range(2):
            mine = jnp.logical_and(sub * half + source == row, sub == source_sub)

            @pl.when(jnp.logical_not(mine))
            def _():
                pltpu.make_async_remote_copy(
                    src_ref=right_send,
                    dst_ref=right_buf.at[source, source_sub],
                    send_sem=send_sem.at[0],
                    recv_sem=recv_sem.at[source, source_sub],
                    device_id={"sub": other},
                    device_id_type=pl.DeviceIdType.MESH,
                ).wait_recv()

    @pl.when(jnp.logical_and(low_far, row == 0))
    def _():
        raw = right_buf[half - 1].astype(jnp.float32).reshape(2 * rows * cols, chan)
        raw = layer_norm(raw, vec_v[0], vec_v[1], -1).astype(jnp.bfloat16)
        far = gated(raw, w_v[:, 0 : 2 * hidden])
        right_buf[half - 1] = far.reshape(2, rows, cols, hidden)

    for source in range(half):
        block = right_buf[source].astype(jnp.float32)
        for i in range(rows):
            prod = left_all[:, i][:, None] * block
            prod = prod[0] + prod[1]
            prod = jnp.sum(prod.reshape(rows, cols // 8, 8, hidden), axis=1)
            tri_v[i, source * rows : (source + 1) * rows, :] = jnp.sum(prod, axis=1)

    tri = tri_v[...].reshape(rows * cols, hidden).astype(jnp.bfloat16).astype(jnp.float32)
    hidden_normed = layer_norm(tri, vec_v[2], vec_v[3], -1).astype(jnp.bfloat16)
    mixed = jnp.dot(hidden_normed, wo_v[...], preferred_element_type=jnp.float32)
    out = (gating.astype(jnp.float32) * mixed).astype(jnp.bfloat16)
    out_ref[...] = out.reshape(rows, cols, chan)

    left_copy.wait_send()
    for q in range(n_row):

        @pl.when(sent[q])
        def _():
            copies[q].wait_send()


def one_round(n_row, pair_rep, norm_gain, norm_bias, *rest):
    w_a_proj, w_a_gate, w_b_proj, w_b_gate, w_gate, out_gain, out_bias, w_out = rest
    rows, cols, chan = pair_rep.shape
    hidden = w_a_proj.shape[1]
    half = n_row // 2
    hbm = pl.BlockSpec(memory_space=pltpu.HBM)
    return pl.pallas_call(
        functools.partial(kernel, n_row),
        out_shape=pltpu.VMEM((rows, cols, chan), jnp.bfloat16),
        in_specs=[hbm] * 11,
        out_specs=pl.BlockSpec(memory_space=pltpu.VMEM),
        scratch_shapes=[
            pltpu.VMEM((rows, cols, chan), jnp.bfloat16),
            pltpu.VMEM((4, 1, chan), jnp.float32),
            pltpu.VMEM((chan, 4 * hidden + chan), jnp.bfloat16),
            pltpu.VMEM((hidden, chan), jnp.bfloat16),
            pltpu.VMEM((rows, cols, hidden), jnp.bfloat16),
            pltpu.VMEM((half, 2, rows, cols, hidden), jnp.bfloat16),
            pltpu.VMEM((2, rows, cols, hidden), jnp.bfloat16),
            pltpu.VMEM((rows, cols, hidden), jnp.float32),
            pltpu.SemaphoreType.DMA((11,)),
            pltpu.SemaphoreType.DMA((n_row + 1,)),
            pltpu.SemaphoreType.DMA((half, 2)),
            pltpu.SemaphoreType.DMA,
            pltpu.SemaphoreType.REGULAR,
            pltpu.SemaphoreType.REGULAR,
        ],
        compiler_params=pltpu.CompilerParams(
            collective_id=0, has_side_effects=True, vmem_limit_bytes=16 * 2**20
        ),
    )(
        *(
            pltpu.with_memory_space_constraint(operand, pltpu.HBM)
            for operand in (
                pair_rep,
                norm_gain.reshape(1, chan),
                norm_bias.reshape(1, chan),
                w_a_proj,
                w_a_gate,
                w_b_proj,
                w_b_gate,
                w_gate,
                out_gain.reshape(1, hidden),
                out_bias.reshape(1, hidden),
                w_out,
            )
        )
    )


def body(n_row, n_sub, *operands):
    rows, cols, chan = operands[0].shape
    hidden = operands[3].shape[1]
    gathered = cols * cols * n_sub * hidden * 2
    if n_sub == 2 and n_row % 2 == 0 and cols % 16 == 0 and hidden == chan and gathered <= 4 * 2**20:
        return one_round(n_row, *operands)
    return per_device(*operands)


def solution(mesh):
    in_specs = (P(("grp", "row"), "sub", None), P(), P(), P(), P(), P(), P(), P(), P(), P(), P())
    out_specs = P(("grp", "row"), "sub", None)
    return jax.shard_map(
        functools.partial(body, mesh.shape["row"], mesh.shape["sub"]),
        mesh=mesh,
        in_specs=in_specs,
        out_specs=out_specs,
        check_vma=False,
    )
```

profile of v0, /device:TPU:1, one launch (start us, length us, event | category | flops | bytes accessed | tf_op | source)
XLA Modules:
  0.0 9.5 jit_solution(1557735857052710385)
XLA Ops:
  0.0 8.9 %shard_map.109 = bf16[4,16,128]{2,1,0:T(8,128)(2,1)S(1)} custom-call(bf16[4,16,128]{2,1,0:T(8,128)(2,1)} %pair_hbm.1, f32[1,128]{1,0:T(1,128)} %bitcast.4, f32[1,128]{1,0:T(1,128)} %bitcast.5, bf16[128,128]{1,0:T(8,128)(2,1)} %wap_hbm.1, bf16[128,128]{1,0:T(8,128)(2,1)} %wag_hbm.1, bf16[128,128]{1,0:T(8,128)(2,1)} %wbp_hbm.1, bf16[128,128]{1,0:T(8,128)(2,1)} %wbg_hbm.1, ...), custom_call_target="tpu_custom_call" | custom-call | tf_op jit(solution)/shard_map/pallas_call | solution.py:373
  8.9 0.6 %copy.13 = bf16[4,16,128]{2,1,0:T(8,128)(2,1)} copy(bf16[4,16,128]{2,1,0:T(8,128)(2,1)S(1)} %shard_map.109) | data formatting | bytes 32768
where the time goes:
time: 9.65 us; the launch traced here: 9.5 us
  Pallas kernels  8.89 us (92%)
  local copies, waits for them, and re-layouts  0.61 us (6%)
    pallas_call x1, Pallas kernels, one_round(): pl.pallas_call(functools.partial(kernel, n_row), out_shape=pltpu.VMEM((ro...  8.89 us
    unnamed x1, local copies, waits for them, and re-layouts  0.61 us

commit v1 on v0

--- a/solution.py
+++ b/solution.py
@@ -132,9 +132,6 @@
         pltpu.make_async_copy(obias_hbm, vec_v.at[3], in_sem.at[9]),
         pltpu.make_async_copy(wo_hbm, wo_v, in_sem.at[10]),
     ]
-    for load in loads:
-        load.start()
-
     barrier = pltpu.get_barrier_semaphore()
 
     def greet(semaphore, target):
@@ -207,16 +204,6 @@
             else:
                 copies[q].start()
 
-    @pl.when(low_near)
-    def _():
-        pl.semaphore_wait(barrier, half)
-        greet(ready, {"sub": 1})
-
-    @pl.when(jnp.logical_and(high_far, mid))
-    def _():
-        pl.semaphore_wait(barrier, half + 1)
-        greet(ready, {"sub": 1})
-
     @pl.when(last)
     def _():
         pl.semaphore_wait(barrier, 2 * half - sub)
@@ -227,6 +214,19 @@
             greet(ready, {"sub": 1})
             for step in range(half):
                 greet(late, {"row": step, "sub": 1})
+
+    for load in loads:
+        load.start()
+
+    @pl.when(low_near)
+    def _():
+        pl.semaphore_wait(barrier, half)
+        greet(ready, {"sub": 1})
+
+    @pl.when(jnp.logical_and(high_far, mid))
+    def _():
+        pl.semaphore_wait(barrier, half + 1)
+        greet(ready, {"sub": 1})
 
     for load in loads[:3]:
         load.wait()

time: 9.65 us -> 9.17 us (0.950)
  Pallas kernels: 8.89 us -> 8.4 us
    pallas_call x1, Pallas kernels: 8.89 us -> 8.4 us  [one_round(): pl.pallas_call(functools.partial(kernel, n_row), out_shape=pltpu.VMEM((ro...]
where the time goes in v1:
time: 9.17 us; the launch traced here: 9.01 us
  Pallas kernels  8.4 us (92%)
  local copies, waits for them, and re-layouts  0.61 us (7%)
    pallas_call x1, Pallas kernels, one_round(): pl.pallas_call(functools.partial(kernel, n_row), out_shape=pltpu.VMEM((ro...  8.4 us
    unnamed x1, local copies, waits for them, and re-layouts  0.61 us

profile of v1, /device:TPU:1, one launch (start us, length us, event | category | flops | bytes accessed | tf_op | source)
XLA Modules:
  0.0 9.0 jit_solution(4848781978246938857)
XLA Ops:
  0.0 8.4 %shard_map.109 = bf16[4,16,128]{2,1,0:T(8,128)(2,1)S(1)} custom-call(bf16[4,16,128]{2,1,0:T(8,128)(2,1)} %pair_hbm.1, f32[1,128]{1,0:T(1,128)} %bitcast.4, f32[1,128]{1,0:T(1,128)} %bitcast.5, bf16[128,128]{1,0:T(8,128)(2,1)} %wap_hbm.1, bf16[128,128]{1,0:T(8,128)(2,1)} %wag_hbm.1, bf16[128,128]{1,0:T(8,128)(2,1)} %wbp_hbm.1, bf16[128,128]{1,0:T(8,128)(2,1)} %wbg_hbm.1, ...), custom_call_target="tpu_custom_call" | custom-call | tf_op jit(solution)/shard_map/pallas_call | solution.py:373
  8.4 0.6 %copy.13 = bf16[4,16,128]{2,1,0:T(8,128)(2,1)} copy(bf16[4,16,128]{2,1,0:T(8,128)(2,1)S(1)} %shard_map.109) | data formatting | bytes 32768

commit v2 on v1

--- a/solution.py
+++ b/solution.py
@@ -65,10 +65,28 @@
     return (gating.astype(jnp.float32) * mixed).astype(jnp.bfloat16)
 
 
-def gated(normed, weights):
+def sigmoid(values):
+    return 0.5 * jnp.tanh(0.5 * values) + 0.5
+
+
+def centre(values, gain):
+    centred = values - jnp.mean(values, axis=-1, keepdims=True)
+    scale = lax.rsqrt(jnp.mean(centred * centred, axis=-1, keepdims=True) + EPSILON)
+    return (centred * gain).astype(jnp.bfloat16), scale
+
+
+def through(shift, weights):
+    high = shift.astype(jnp.bfloat16)
+    low = (shift - high.astype(jnp.float32)).astype(jnp.bfloat16)
+    pair = jnp.concatenate([jnp.broadcast_to(high, (8, high.shape[1])), jnp.broadcast_to(low, (8, low.shape[1]))], axis=0)
+    mixed = jnp.dot(pair, weights, preferred_element_type=jnp.float32)
+    return mixed[0:1] + mixed[8:9]
+
+
+def gated(centred, scale, shift, weights):
     hidden = weights.shape[1] // 2
-    inner = jnp.dot(normed, weights, preferred_element_type=jnp.float32)
-    return (jax.nn.sigmoid(inner[:, hidden:]) * inner[:, :hidden]).astype(jnp.bfloat16)
+    inner = jnp.dot(centred, weights, preferred_element_type=jnp.float32) * scale + shift
+    return (sigmoid(inner[:, hidden:]) * inner[:, :hidden]).astype(jnp.bfloat16)
 
 
 def kernel(
@@ -116,6 +134,8 @@
     high_far = jnp.logical_and(owner == 1, sub == 0)
     last = row == n_row - 1
     split = half // 2
+    order = [half + q for pair in zip(range(split), range(split, half - 1)) for q in pair]
+    order += [q for q in range(half, n_row - 1) if q not in order]
     mid = jnp.logical_and(owner == 1, slot < split)
     outer = jnp.logical_and(owner == 1, jnp.logical_and(slot >= split, jnp.logical_not(last)))
 
@@ -189,9 +209,6 @@
 
     raw_copy = block_copy(pair_hbm, 0, 0, owner)
     copies = [block_copy(right_send, q, q, owner) for q in range(n_row)]
-    copies[half:] = [
-        block_copy(right_send, q, q, jnp.where(low, 0, 1)) for q in range(half, n_row)
-    ]
     sent = [jnp.logical_not(jnp.logical_and(near, row == q)) for q in range(n_row)]
 
     def start(first, end, guarded):
@@ -231,10 +248,12 @@
     for load in loads[:3]:
         load.wait()
     pair = pair_v[...].astype(jnp.float32).reshape(rows * cols, chan)
-    normed = layer_norm(pair, vec_v[0], vec_v[1], -1).astype(jnp.bfloat16)
+    centred, scale = centre(pair, vec_v[0])
     for load in loads[3:5]:
         load.wait()
-    right = gated(normed, w_v[:, 0 : 2 * hidden]).reshape(rows, cols, hidden)
+    right_shift = through(vec_v[1], w_v[:, 0 : 2 * hidden])
+    right = gated(centred, scale, right_shift, w_v[:, 0 : 2 * hidden])
+    right = right.reshape(rows, cols, hidden)
     right_send[...] = right
 
     @pl.when(low_far)
@@ -265,7 +284,8 @@
 
     for load in loads[5:7]:
         load.wait()
-    left = gated(normed, w_v[:, 2 * hidden : 4 * hidden])
+    left_shift = through(vec_v[1], w_v[:, 2 * hidden : 4 * hidden])
+    left = gated(centred, scale, left_shift, w_v[:, 2 * hidden : 4 * hidden])
     left_buf[sub] = left.reshape(rows, cols, hidden)
 
     @pl.when(jnp.logical_and(high_near, jnp.logical_not(mid)))
@@ -288,13 +308,12 @@
         start(half, n_row, True)
 
     loads[7].wait()
-    gating = jax.nn.sigmoid(
-        jnp.dot(
-            normed, w_v[:, 4 * hidden : 4 * hidden + chan], preferred_element_type=jnp.float32
-        )
-    ).astype(jnp.bfloat16)
+    gate = w_v[:, 4 * hidden : 4 * hidden + chan]
+    gating = jnp.dot(centred, gate, preferred_element_type=jnp.float32) * scale
+    gating = sigmoid(gating + through(vec_v[1], gate)).astype(jnp.bfloat16)
     for load in loads[8:]:
         load.wait()
+    out_shift = through(vec_v[3], wo_v[...])
 
     @pl.when(low_far)
     def _():
@@ -307,7 +326,8 @@
 
     @pl.when(low)
     def _():
-        start(half, n_row - 1, False)
+        for q in order:
+            copies[q].start()
         pl.semaphore_wait(late, 1)
 
     @pl.when(low_far)
@@ -319,40 +339,62 @@
         copies[-1].start()
 
     left_copy.wait_recv()
-    left_all = left_buf[...].astype(jnp.float32)
-    for source in range(half):
-        for source_sub in range(2):
-            mine = jnp.logical_and(sub * half + source == row, sub == source_sub)
-
-            @pl.when(jnp.logical_not(mine))
-            def _():
-                pltpu.make_async_remote_copy(
-                    src_ref=right_send,
-                    dst_ref=right_buf.at[source, source_sub],
-                    send_sem=send_sem.at[0],
-                    recv_sem=recv_sem.at[source, source_sub],
-                    device_id={"sub": other},
-                    device_id_type=pl.DeviceIdType.MESH,
-                ).wait_recv()
-
-    @pl.when(jnp.logical_and(low_far, row == 0))
-    def _():
-        raw = right_buf[half - 1].astype(jnp.float32).reshape(2 * rows * cols, chan)
-        raw = layer_norm(raw, vec_v[0], vec_v[1], -1).astype(jnp.bfloat16)
-        far = gated(raw, w_v[:, 0 : 2 * hidden])
-        right_buf[half - 1] = far.reshape(2, rows, cols, hidden)
-
-    for source in range(half):
-        block = right_buf[source].astype(jnp.float32)
+
+    def arrive(source, source_sub):
+        return pltpu.make_async_remote_copy(
+            src_ref=right_send,
+            dst_ref=right_buf.at[source, source_sub],
+            send_sem=send_sem.at[0],
+            recv_sem=recv_sem.at[source, source_sub],
+            device_id={"sub": other},
+            device_id_type=pl.DeviceIdType.MESH,
+        )
+
+    def absorb(source, block):
         for i in range(rows):
-            prod = left_all[:, i][:, None] * block
+            prod = left_buf[:, i].astype(jnp.float32)[:, None] * block
             prod = prod[0] + prod[1]
             prod = jnp.sum(prod.reshape(rows, cols // 8, 8, hidden), axis=1)
             tri_v[i, source * rows : (source + 1) * rows, :] = jnp.sum(prod, axis=1)
 
+    def project(source):
+        raw = right_buf[source].astype(jnp.float32).reshape(2 * rows * cols, chan)
+        raw_centred, raw_scale = centre(raw, vec_v[0])
+        far = gated(raw_centred, raw_scale, right_shift, w_v[:, 0 : 2 * hidden])
+        return far.astype(jnp.float32).reshape(2, rows, cols, hidden)
+
+    first = jnp.logical_and(low_far, row == 0)
+
+    @pl.when(first)
+    def _():
+        for group in [list(range(half // 2)), list(range(half // 2, half))]:
+            for source in group:
+                for source_sub in range(2):
+                    arrive(source, source_sub).wait_recv()
+            for source in group[::-1]:
+                if source == half - 1:
+                    absorb(source, project(source))
+                else:
+                    absorb(source, right_buf[source].astype(jnp.float32))
+
+    @pl.when(jnp.logical_not(first))
+    def _():
+        for group in [list(range(half // 2)), list(range(half // 2, half))]:
+            for source in group:
+                for source_sub in range(2):
+                    mine = jnp.logical_and(sub * half + source == row, sub == source_sub)
+
+                    @pl.when(jnp.logical_not(mine))
+                    def _():
+                        arrive(source, source_sub).wait_recv()
+
+            for source in group:
+                absorb(source, right_buf[source].astype(jnp.float32))
+
     tri = tri_v[...].reshape(rows * cols, hidden).astype(jnp.bfloat16).astype(jnp.float32)
-    hidden_normed = layer_norm(tri, vec_v[2], vec_v[3], -1).astype(jnp.bfloat16)
-    mixed = jnp.dot(hidden_normed, wo_v[...], preferred_element_type=jnp.float32)
+    tri_centred, tri_scale = centre(tri, vec_v[2])
+    mixed = jnp.dot(tri_centred, wo_v[...], preferred_element_type=jnp.float32)
+    mixed = mixed * tri_scale + out_shift
     out = (gating.astype(jnp.float32) * mixed).astype(jnp.bfloat16)
     out_ref[...] = out.reshape(rows, cols, chan)
 

time: 9.17 us -> 8.97 us (0.978)
  Pallas kernels: 8.4 us -> 8.19 us
    pallas_call x1, Pallas kernels: 8.4 us -> 8.19 us  [one_round(): pl.pallas_call(functools.partial(kernel, n_row), out_shape=pltpu.VMEM((ro...]
where the time goes in v2:
time: 8.97 us; the launch traced here: 8.81 us
  Pallas kernels  8.19 us (91%)
  local copies, waits for them, and re-layouts  0.61 us (7%)
    pallas_call x1, Pallas kernels, one_round(): pl.pallas_call(functools.partial(kernel, n_row), out_shape=pltpu.VMEM((ro...  8.19 us
    unnamed x1, local copies, waits for them, and re-layouts  0.61 us

profile of v2, /device:TPU:1, one launch (start us, length us, event | category | flops | bytes accessed | tf_op | source)
XLA Modules:
  0.0 8.8 jit_solution(11815384372255506111)
XLA Ops:
  0.0 8.2 %shard_map.109 = bf16[4,16,128]{2,1,0:T(8,128)(2,1)S(1)} custom-call(bf16[4,16,128]{2,1,0:T(8,128)(2,1)} %pair_hbm.1, f32[1,128]{1,0:T(1,128)} %bitcast.4, f32[1,128]{1,0:T(1,128)} %bitcast.5, bf16[128,128]{1,0:T(8,128)(2,1)} %wap_hbm.1, bf16[128,128]{1,0:T(8,128)(2,1)} %wag_hbm.1, bf16[128,128]{1,0:T(8,128)(2,1)} %wbp_hbm.1, bf16[128,128]{1,0:T(8,128)(2,1)} %wbg_hbm.1, ...), custom_call_target="tpu_custom_call" | custom-call | tf_op jit(solution)/shard_map/pallas_call | solution.py:415
  8.2 0.6 %copy.13 = bf16[4,16,128]{2,1,0:T(8,128)(2,1)} copy(bf16[4,16,128]{2,1,0:T(8,128)(2,1)S(1)} %shard_map.109) | data formatting | bytes 32768

commit v3 on v2

--- a/solution.py
+++ b/solution.py
@@ -106,7 +106,6 @@
     pair_v,
     vec_v,
     w_v,
-    wo_v,
     right_send,
     right_buf,
     left_buf,
@@ -139,19 +138,17 @@
     mid = jnp.logical_and(owner == 1, slot < split)
     outer = jnp.logical_and(owner == 1, jnp.logical_and(slot >= split, jnp.logical_not(last)))
 
-    loads = [
-        pltpu.make_async_copy(pair_hbm, pair_v, in_sem.at[0]),
-        pltpu.make_async_copy(ngain_hbm, vec_v.at[0], in_sem.at[1]),
-        pltpu.make_async_copy(nbias_hbm, vec_v.at[1], in_sem.at[2]),
-        pltpu.make_async_copy(wbp_hbm, w_v.at[:, 0:hidden], in_sem.at[3]),
-        pltpu.make_async_copy(wbg_hbm, w_v.at[:, hidden : 2 * hidden], in_sem.at[4]),
-        pltpu.make_async_copy(wap_hbm, w_v.at[:, 2 * hidden : 3 * hidden], in_sem.at[5]),
-        pltpu.make_async_copy(wag_hbm, w_v.at[:, 3 * hidden : 4 * hidden], in_sem.at[6]),
-        pltpu.make_async_copy(wg_hbm, w_v.at[:, 4 * hidden : 4 * hidden + chan], in_sem.at[7]),
-        pltpu.make_async_copy(ogain_hbm, vec_v.at[2], in_sem.at[8]),
-        pltpu.make_async_copy(obias_hbm, vec_v.at[3], in_sem.at[9]),
-        pltpu.make_async_copy(wo_hbm, wo_v, in_sem.at[10]),
-    ]
+    weights = (wbp_hbm, wbg_hbm, wap_hbm, wag_hbm, wg_hbm, wo_hbm)
+    loads = [pltpu.make_async_copy(pair_hbm, pair_v, in_sem.at[0])]
+    for n, vector in enumerate((ngain_hbm, nbias_hbm, ogain_hbm, obias_hbm)):
+        loads.append(pltpu.make_async_copy(vector, vec_v.at[n], in_sem.at[1]))
+    for n, weight in enumerate(weights):
+        span = w_v.at[:, n * hidden : (n + 1) * hidden]
+        loads.append(pltpu.make_async_copy(weight, span, in_sem.at[2 if n < 2 else 3]))
+
+    def loaded(span, index):
+        pltpu.make_async_copy(span, span, in_sem.at[index]).wait()
+
     barrier = pltpu.get_barrier_semaphore()
 
     def greet(semaphore, target):
@@ -191,24 +188,24 @@
     left_copy = pltpu.make_async_remote_copy(
         src_ref=left_buf.at[sub],
         dst_ref=left_buf.at[sub],
-        send_sem=send_sem.at[n_row],
+        send_sem=send_sem.at[1],
         recv_sem=left_sem,
         device_id={"sub": other},
         device_id_type=pl.DeviceIdType.MESH,
     )
 
-    def block_copy(source, index, target_row, target_sub):
+    def block_copy(source, target_row, target_sub):
         return pltpu.make_async_remote_copy(
             src_ref=source,
-            dst_ref=right_buf.at[slot, sub],
-            send_sem=send_sem.at[index],
-            recv_sem=recv_sem.at[slot, sub],
+            dst_ref=right_buf.at[2 * slot + sub],
+            send_sem=send_sem.at[0],
+            recv_sem=recv_sem.at[slot // split],
             device_id={"row": target_row, "sub": target_sub},
             device_id_type=pl.DeviceIdType.MESH,
         )
 
-    raw_copy = block_copy(pair_hbm, 0, 0, owner)
-    copies = [block_copy(right_send, q, q, owner) for q in range(n_row)]
+    raw_copy = block_copy(pair_hbm, 0, owner)
+    copies = [block_copy(right_send, q, owner) for q in range(n_row)]
     sent = [jnp.logical_not(jnp.logical_and(near, row == q)) for q in range(n_row)]
 
     def start(first, end, guarded):
@@ -245,12 +242,11 @@
         pl.semaphore_wait(barrier, half + 1)
         greet(ready, {"sub": 1})
 
-    for load in loads[:3]:
-        load.wait()
+    loaded(pair_v, 0)
+    loaded(vec_v, 1)
     pair = pair_v[...].astype(jnp.float32).reshape(rows * cols, chan)
     centred, scale = centre(pair, vec_v[0])
-    for load in loads[3:5]:
-        load.wait()
+    loaded(w_v.at[:, 0 : 2 * hidden], 2)
     right_shift = through(vec_v[1], w_v[:, 0 : 2 * hidden])
     right = gated(centred, scale, right_shift, w_v[:, 0 : 2 * hidden])
     right = right.reshape(rows, cols, hidden)
@@ -280,10 +276,9 @@
 
     @pl.when(near)
     def _():
-        right_buf[slot, sub] = right
-
-    for load in loads[5:7]:
-        load.wait()
+        right_buf[2 * slot + sub] = right
+
+    loaded(w_v.at[:, 2 * hidden :], 3)
     left_shift = through(vec_v[1], w_v[:, 2 * hidden : 4 * hidden])
     left = gated(centred, scale, left_shift, w_v[:, 2 * hidden : 4 * hidden])
     left_buf[sub] = left.reshape(rows, cols, hidden)
@@ -307,13 +302,11 @@
     def _():
         start(half, n_row, True)
 
-    loads[7].wait()
     gate = w_v[:, 4 * hidden : 4 * hidden + chan]
     gating = jnp.dot(centred, gate, preferred_element_type=jnp.float32) * scale
     gating = sigmoid(gating + through(vec_v[1], gate)).astype(jnp.bfloat16)
-    for load in loads[8:]:
-        load.wait()
-    out_shift = through(vec_v[3], wo_v[...])
+    w_out = w_v[:, 5 * hidden : 6 * hidden]
+    out_shift = through(vec_v[3], w_out)
 
     @pl.when(low_far)
     def _():
@@ -340,15 +333,18 @@
 
     left_copy.wait_recv()
 
-    def arrive(source, source_sub):
-        return pltpu.make_async_remote_copy(
-            src_ref=right_send,
-            dst_ref=right_buf.at[source, source_sub],
+    def arrived(group, blocks):
+        pltpu.make_async_remote_copy(
+            src_ref=right_buf.at[0:blocks],
+            dst_ref=right_buf.at[0:blocks],
             send_sem=send_sem.at[0],
-            recv_sem=recv_sem.at[source, source_sub],
+            recv_sem=recv_sem.at[group],
             device_id={"sub": other},
             device_id_type=pl.DeviceIdType.MESH,
-        )
+        ).wait_recv()
+
+    def block_of(source):
+        return right_buf[2 * source : 2 * source + 2].astype(jnp.float32)
 
     def absorb(source, block):
         for i in range(rows):
@@ -358,7 +354,7 @@
             tri_v[i, source * rows : (source + 1) * rows, :] = jnp.sum(prod, axis=1)
 
     def project(source):
-        raw = right_buf[source].astype(jnp.float32).reshape(2 * rows * cols, chan)
+        raw = block_of(source).reshape(2 * rows * cols, chan)
         raw_centred, raw_scale = centre(raw, vec_v[0])
         far = gated(raw_centred, raw_scale, right_shift, w_v[:, 0 : 2 * hidden])
         return far.astype(jnp.float32).reshape(2, rows, cols, hidden)
@@ -367,43 +363,55 @@
 
     @pl.when(first)
     def _():
-        for group in [list(range(half // 2)), list(range(half // 2, half))]:
-            for source in group:
-                for source_sub in range(2):
-                    arrive(source, source_sub).wait_recv()
-            for source in group[::-1]:
-                if source == half - 1:
-                    absorb(source, project(source))
-                else:
-                    absorb(source, right_buf[source].astype(jnp.float32))
+        arrived(0, 2 * split)
+        for source in range(split):
+            absorb(source, block_of(source))
+        arrived(1, 2 * split)
+        absorb(half - 1, project(half - 1))
+        for source in range(split, half - 1):
+            absorb(source, block_of(source))
 
     @pl.when(jnp.logical_not(first))
     def _():
-        for group in [list(range(half // 2)), list(range(half // 2, half))]:
-            for source in group:
-                for source_sub in range(2):
-                    mine = jnp.logical_and(sub * half + source == row, sub == source_sub)
-
-                    @pl.when(jnp.logical_not(mine))
-                    def _():
-                        arrive(source, source_sub).wait_recv()
-
-            for source in group:
-                absorb(source, right_buf[source].astype(jnp.float32))
+        for group in range(2):
+            own = jnp.logical_and(near, slot // split == group)
+
+            @pl.when(own)
+            def _():
+                arrived(group, 2 * split - 1)
+
+            @pl.when(jnp.logical_not(own))
+            def _():
+                arrived(group, 2 * split)
+
+            for source in range(group * split, (group + 1) * split):
+                absorb(source, block_of(source))
 
     tri = tri_v[...].reshape(rows * cols, hidden).astype(jnp.bfloat16).astype(jnp.float32)
     tri_centred, tri_scale = centre(tri, vec_v[2])
-    mixed = jnp.dot(tri_centred, wo_v[...], preferred_element_type=jnp.float32)
+    mixed = jnp.dot(tri_centred, w_out, preferred_element_type=jnp.float32)
     mixed = mixed * tri_scale + out_shift
     out = (gating.astype(jnp.float32) * mixed).astype(jnp.bfloat16)
     out_ref[...] = out.reshape(rows, cols, chan)
 
     left_copy.wait_send()
-    for q in range(n_row):
-
-        @pl.when(sent[q])
-        def _():
-            copies[q].wait_send()
+    def gone(blocks):
+        pltpu.make_async_remote_copy(
+            src_ref=right_buf.at[0:blocks],
+            dst_ref=right_buf.at[0:blocks],
+            send_sem=send_sem.at[0],
+            recv_sem=recv_sem.at[0],
+            device_id={"sub": other},
+            device_id_type=pl.DeviceIdType.MESH,
+        ).wait_send()
+
+    @pl.when(near)
+    def _():
+        gone(n_row - 1)
+
+    @pl.when(jnp.logical_not(near))
+    def _():
+        gone(n_row)
 
 
 def one_round(n_row, pair_rep, norm_gain, norm_bias, *rest):
@@ -420,15 +428,14 @@
         scratch_shapes=[
             pltpu.VMEM((rows, cols, chan), jnp.bfloat16),
             pltpu.VMEM((4, 1, chan), jnp.float32),
-            pltpu.VMEM((chan, 4 * hidden + chan), jnp.bfloat16),
-            pltpu.VMEM((hidden, chan), jnp.bfloat16),
+            pltpu.VMEM((chan, 6 * hidden), jnp.bfloat16),
             pltpu.VMEM((rows, cols, hidden), jnp.bfloat16),
-            pltpu.VMEM((half, 2, rows, cols, hidden), jnp.bfloat16),
+            pltpu.VMEM((2 * half, rows, cols, hidden), jnp.bfloat16),
             pltpu.VMEM((2, rows, cols, hidden), jnp.bfloat16),
             pltpu.VMEM((rows, cols, hidden), jnp.float32),
-            pltpu.SemaphoreType.DMA((11,)),
-            pltpu.SemaphoreType.DMA((n_row + 1,)),
-            pltpu.SemaphoreType.DMA((half, 2)),
+            pltpu.SemaphoreType.DMA((4,)),
+            pltpu.SemaphoreType.DMA((2,)),
+            pltpu.SemaphoreType.DMA((2,)),
             pltpu.SemaphoreType.DMA,
             pltpu.SemaphoreType.REGULAR,
             pltpu.SemaphoreType.REGULAR,
@@ -460,7 +467,7 @@
     rows, cols, chan = operands[0].shape
     hidden = operands[3].shape[1]
     gathered = cols * cols * n_sub * hidden * 2
-    if n_sub == 2 and n_row % 2 == 0 and cols % 16 == 0 and hidden == chan and gathered <= 4 * 2**20:
+    if n_sub == 2 and n_row % 4 == 0 and cols % 16 == 0 and hidden == chan and gathered <= 4 * 2**20:
         return one_round(n_row, *operands)
     return per_device(*operands)
 

time: 8.97 us -> 8.76 us (0.977)
  Pallas kernels: 8.19 us -> 7.99 us
    pallas_call x1, Pallas kernels: 8.19 us -> 7.99 us  [one_round(): pl.pallas_call(functools.partial(kernel, n_row), out_shape=pltpu.VMEM((ro...]
where the time goes in v3:
time: 8.76 us; the launch traced here: 8.61 us
  Pallas kernels  7.99 us (91%)
  local copies, waits for them, and re-layouts  0.61 us (7%)
    pallas_call x1, Pallas kernels, one_round(): pl.pallas_call(functools.partial(kernel, n_row), out_shape=pltpu.VMEM((ro...  7.99 us
    unnamed x1, local copies, waits for them, and re-layouts  0.61 us

profile of v3, /device:TPU:1, one launch (start us, length us, event | category | flops | bytes accessed | tf_op | source)
XLA Modules:
  0.0 8.6 jit_solution(18435403637826723108)
XLA Ops:
  0.0 8.0 %shard_map.109 = bf16[4,16,128]{2,1,0:T(8,128)(2,1)S(1)} custom-call(bf16[4,16,128]{2,1,0:T(8,128)(2,1)} %pair_hbm.1, f32[1,128]{1,0:T(1,128)} %bitcast.4, f32[1,128]{1,0:T(1,128)} %bitcast.5, bf16[128,128]{1,0:T(8,128)(2,1)} %wap_hbm.1, bf16[128,128]{1,0:T(8,128)(2,1)} %wag_hbm.1, bf16[128,128]{1,0:T(8,128)(2,1)} %wbp_hbm.1, bf16[128,128]{1,0:T(8,128)(2,1)} %wbg_hbm.1, ...), custom_call_target="tpu_custom_call" | custom-call | tf_op jit(solution)/shard_map/pallas_call | solution.py:423
  8.0 0.6 %copy.13 = bf16[4,16,128]{2,1,0:T(8,128)(2,1)} copy(bf16[4,16,128]{2,1,0:T(8,128)(2,1)S(1)} %shard_map.109) | data formatting | bytes 32768

commit v4 on v3

--- a/solution.py
+++ b/solution.py
@@ -113,9 +113,10 @@
     in_sem,
     send_sem,
     recv_sem,
-    left_sem,
     ready,
     late,
+    bytes_v,
+    fold_v,
 ):
     rows, cols, chan = pair_v.shape
     hidden = right_send.shape[-1]
@@ -132,6 +133,7 @@
     high_near = jnp.logical_and(owner == 1, sub == 1)
     high_far = jnp.logical_and(owner == 1, sub == 0)
     last = row == n_row - 1
+    first = jnp.logical_and(low_far, row == 0)
     split = half // 2
     order = [half + q for pair in zip(range(split), range(split, half - 1)) for q in pair]
     order += [q for q in range(half, n_row - 1) if q not in order]
@@ -141,10 +143,10 @@
     weights = (wbp_hbm, wbg_hbm, wap_hbm, wag_hbm, wg_hbm, wo_hbm)
     loads = [pltpu.make_async_copy(pair_hbm, pair_v, in_sem.at[0])]
     for n, vector in enumerate((ngain_hbm, nbias_hbm, ogain_hbm, obias_hbm)):
-        loads.append(pltpu.make_async_copy(vector, vec_v.at[n], in_sem.at[1]))
+        loads.append(pltpu.make_async_copy(vector, vec_v.at[n], in_sem.at[0]))
     for n, weight in enumerate(weights):
         span = w_v.at[:, n * hidden : (n + 1) * hidden]
-        loads.append(pltpu.make_async_copy(weight, span, in_sem.at[2 if n < 2 else 3]))
+        loads.append(pltpu.make_async_copy(weight, span, in_sem.at[1 if n < 2 else 2]))
 
     def loaded(span, index):
         pltpu.make_async_copy(span, span, in_sem.at[index]).wait()
@@ -156,10 +158,38 @@
             semaphore, inc=1, device_id=target, device_id_type=pl.DeviceIdType.MESH
         )
 
-    @pl.when(low_near)
-    def _():
-        for step in range(1, half):
-            greet(barrier, {"row": lax.rem(slot + step, half), "sub": 0})
+    left_copy = pltpu.make_async_remote_copy(
+        src_ref=left_buf.at[sub],
+        dst_ref=left_buf.at[sub],
+        send_sem=in_sem.at[0],
+        recv_sem=recv_sem.at[0],
+        device_id={"sub": other},
+        device_id_type=pl.DeviceIdType.MESH,
+    )
+
+    def block_copy(source, target_row, target_sub):
+        return pltpu.make_async_remote_copy(
+            src_ref=source,
+            dst_ref=right_buf.at[2 * slot + sub],
+            send_sem=send_sem,
+            recv_sem=recv_sem.at[slot // split],
+            device_id={"row": target_row, "sub": target_sub},
+            device_id_type=pl.DeviceIdType.MESH,
+        )
+
+    raw_copy = block_copy(pair_hbm, 0, owner)
+    copies = [block_copy(right_send, q, owner) for q in range(n_row)]
+    sent = [jnp.logical_not(jnp.logical_and(near, row == q)) for q in range(n_row)]
+
+    def start(first, end, guarded):
+        for q in range(first, end):
+            if guarded:
+
+                @pl.when(sent[q])
+                def _():
+                    copies[q].start()
+            else:
+                copies[q].start()
 
     @pl.when(low_far)
     def _():
@@ -169,11 +199,6 @@
             if step >= split:
                 greet(barrier, {"row": half + step, "sub": 1})
 
-    @pl.when(jnp.logical_and(high_far, jnp.logical_not(last)))
-    def _():
-        for step in range(half):
-            greet(barrier, {"row": step, "sub": 1})
-
     @pl.when(high_near)
     def _():
         greet(barrier, {"sub": 0})
@@ -185,39 +210,6 @@
                 if step >= split:
                     greet(barrier, {"row": half + step, "sub": 0})
 
-    left_copy = pltpu.make_async_remote_copy(
-        src_ref=left_buf.at[sub],
-        dst_ref=left_buf.at[sub],
-        send_sem=send_sem.at[1],
-        recv_sem=left_sem,
-        device_id={"sub": other},
-        device_id_type=pl.DeviceIdType.MESH,
-    )
-
-    def block_copy(source, target_row, target_sub):
-        return pltpu.make_async_remote_copy(
-            src_ref=source,
-            dst_ref=right_buf.at[2 * slot + sub],
-            send_sem=send_sem.at[0],
-            recv_sem=recv_sem.at[slot // split],
-            device_id={"row": target_row, "sub": target_sub},
-            device_id_type=pl.DeviceIdType.MESH,
-        )
-
-    raw_copy = block_copy(pair_hbm, 0, owner)
-    copies = [block_copy(right_send, q, owner) for q in range(n_row)]
-    sent = [jnp.logical_not(jnp.logical_and(near, row == q)) for q in range(n_row)]
-
-    def start(first, end, guarded):
-        for q in range(first, end):
-            if guarded:
-
-                @pl.when(sent[q])
-                def _():
-                    copies[q].start()
-            else:
-                copies[q].start()
-
     @pl.when(last)
     def _():
         pl.semaphore_wait(barrier, 2 * half - sub)
@@ -229,6 +221,16 @@
             for step in range(half):
                 greet(late, {"row": step, "sub": 1})
 
+    @pl.when(jnp.logical_and(high_far, jnp.logical_not(last)))
+    def _():
+        for step in range(half):
+            greet(barrier, {"row": step, "sub": 1})
+
+    @pl.when(low_near)
+    def _():
+        for step in range(1, half):
+            greet(barrier, {"row": lax.rem(slot + step, half), "sub": 0})
+
     for load in loads:
         load.start()
 
@@ -242,11 +244,10 @@
         pl.semaphore_wait(barrier, half + 1)
         greet(ready, {"sub": 1})
 
-    loaded(pair_v, 0)
-    loaded(vec_v, 1)
+    loaded(bytes_v, 0)
     pair = pair_v[...].astype(jnp.float32).reshape(rows * cols, chan)
     centred, scale = centre(pair, vec_v[0])
-    loaded(w_v.at[:, 0 : 2 * hidden], 2)
+    loaded(w_v.at[:, 0 : 2 * hidden], 1)
     right_shift = through(vec_v[1], w_v[:, 0 : 2 * hidden])
     right = gated(centred, scale, right_shift, w_v[:, 0 : 2 * hidden])
     right = right.reshape(rows, cols, hidden)
@@ -278,7 +279,7 @@
     def _():
         right_buf[2 * slot + sub] = right
 
-    loaded(w_v.at[:, 2 * hidden :], 3)
+    loaded(w_v.at[:, 2 * hidden :], 2)
     left_shift = through(vec_v[1], w_v[:, 2 * hidden : 4 * hidden])
     left = gated(centred, scale, left_shift, w_v[:, 2 * hidden : 4 * hidden])
     left_buf[sub] = left.reshape(rows, cols, hidden)
@@ -305,6 +306,15 @@
     gate = w_v[:, 4 * hidden : 4 * hidden + chan]
     gating = jnp.dot(centred, gate, preferred_element_type=jnp.float32) * scale
     gating = sigmoid(gating + through(vec_v[1], gate)).astype(jnp.bfloat16)
+    @pl.when(first)
+    def _():
+        gain = jnp.broadcast_to(vec_v[0], (chan, chan)).T[:, 0:1]
+        folded = w_v[:, 0 : 2 * hidden].astype(jnp.float32) * gain
+        folded = folded - jnp.mean(folded, axis=0, keepdims=True)
+        high = folded.astype(jnp.bfloat16)
+        fold_v[0:chan] = high
+        fold_v[chan:] = (folded - high.astype(jnp.float32)).astype(jnp.bfloat16)
+
     w_out = w_v[:, 5 * hidden : 6 * hidden]
     out_shift = through(vec_v[3], w_out)
 
@@ -331,13 +341,12 @@
     def _():
         copies[-1].start()
 
-    left_copy.wait_recv()
 
     def arrived(group, blocks):
         pltpu.make_async_remote_copy(
             src_ref=right_buf.at[0:blocks],
             dst_ref=right_buf.at[0:blocks],
-            send_sem=send_sem.at[0],
+            send_sem=send_sem,
             recv_sem=recv_sem.at[group],
             device_id={"sub": other},
             device_id_type=pl.DeviceIdType.MESH,
@@ -354,16 +363,18 @@
             tri_v[i, source * rows : (source + 1) * rows, :] = jnp.sum(prod, axis=1)
 
     def project(source):
-        raw = block_of(source).reshape(2 * rows * cols, chan)
-        raw_centred, raw_scale = centre(raw, vec_v[0])
-        far = gated(raw_centred, raw_scale, right_shift, w_v[:, 0 : 2 * hidden])
+        bits = right_buf[2 * source : 2 * source + 2].reshape(2 * rows * cols, chan)
+        raw = bits.astype(jnp.float32)
+        moved = raw - jnp.mean(raw, axis=-1, keepdims=True)
+        raw_scale = lax.rsqrt(jnp.mean(moved * moved, axis=-1, keepdims=True) + EPSILON)
+        twice = jnp.concatenate([bits, bits], axis=1)
+        far = gated(twice, raw_scale, right_shift, fold_v[...])
         return far.astype(jnp.float32).reshape(2, rows, cols, hidden)
 
-    first = jnp.logical_and(low_far, row == 0)
 
     @pl.when(first)
     def _():
-        arrived(0, 2 * split)
+        arrived(0, 2 * split + 1)
         for source in range(split):
             absorb(source, block_of(source))
         arrived(1, 2 * split)
@@ -378,11 +389,11 @@
 
             @pl.when(own)
             def _():
-                arrived(group, 2 * split - 1)
+                arrived(group, 2 * split - group)
 
             @pl.when(jnp.logical_not(own))
             def _():
-                arrived(group, 2 * split)
+                arrived(group, 2 * split + 1 - group)
 
             for source in range(group * split, (group + 1) * split):
                 absorb(source, block_of(source))
@@ -399,7 +410,7 @@
         pltpu.make_async_remote_copy(
             src_ref=right_buf.at[0:blocks],
             dst_ref=right_buf.at[0:blocks],
-            send_sem=send_sem.at[0],
+            send_sem=send_sem,
             recv_sem=recv_sem.at[0],
             device_id={"sub": other},
             device_id_type=pl.DeviceIdType.MESH,
@@ -433,12 +444,13 @@
             pltpu.VMEM((2 * half, rows, cols, hidden), jnp.bfloat16),
             pltpu.VMEM((2, rows, cols, hidden), jnp.bfloat16),
             pltpu.VMEM((rows, cols, hidden), jnp.float32),
-            pltpu.SemaphoreType.DMA((4,)),
+            pltpu.SemaphoreType.DMA((3,)),
+            pltpu.SemaphoreType.DMA,
             pltpu.SemaphoreType.DMA((2,)),
-            pltpu.SemaphoreType.DMA((2,)),
-            pltpu.SemaphoreType.DMA,
             pltpu.SemaphoreType.REGULAR,
             pltpu.SemaphoreType.REGULAR,
+            pltpu.VMEM((rows * cols + 8, chan), jnp.bfloat16),
+            pltpu.VMEM((2 * chan, 2 * hidden), jnp.bfloat16),
         ],
         compiler_params=pltpu.CompilerParams(
             collective_id=0, has_side_effects=True, vmem_limit_bytes=16 * 2**20

time: 8.76 us -> 8.7 us (level)
  no operation moved by 1% of the time
where the time goes in v4:
time: 8.7 us; the launch traced here: 8.55 us
  Pallas kernels  7.93 us (91%)
  local copies, waits for them, and re-layouts  0.61 us (7%)
    pallas_call x1, Pallas kernels, one_round(): pl.pallas_call(functools.partial(kernel, n_row), out_shape=pltpu.VMEM((ro...  7.93 us
    unnamed x1, local copies, waits for them, and re-layouts  0.61 us

profile of v4, /device:TPU:1, one launch (start us, length us, event | category | flops | bytes accessed | tf_op | source)
XLA Modules:
  0.0 8.5 jit_solution(8595103546837279645)
XLA Ops:
  0.0 7.9 %shard_map.109 = bf16[4,16,128]{2,1,0:T(8,128)(2,1)S(1)} custom-call(bf16[4,16,128]{2,1,0:T(8,128)(2,1)} %pair_hbm.1, f32[1,128]{1,0:T(1,128)} %bitcast.4, f32[1,128]{1,0:T(1,128)} %bitcast.5, bf16[128,128]{1,0:T(8,128)(2,1)} %wap_hbm.1, bf16[128,128]{1,0:T(8,128)(2,1)} %wag_hbm.1, bf16[128,128]{1,0:T(8,128)(2,1)} %wbp_hbm.1, bf16[128,128]{1,0:T(8,128)(2,1)} %wbg_hbm.1, ...), custom_call_target="tpu_custom_call" | custom-call | tf_op jit(solution)/shard_map/pallas_call | solution.py:434
  7.9 0.6 %copy.13 = bf16[4,16,128]{2,1,0:T(8,128)(2,1)} copy(bf16[4,16,128]{2,1,0:T(8,128)(2,1)S(1)} %shard_map.109) | data formatting | bytes 32768

commit v5 on v4

--- a/solution.py
+++ b/solution.py
@@ -449,7 +449,7 @@
             pltpu.SemaphoreType.DMA((2,)),
             pltpu.SemaphoreType.REGULAR,
             pltpu.SemaphoreType.REGULAR,
-            pltpu.VMEM((rows * cols + 8, chan), jnp.bfloat16),
+            pltpu.VMEM((rows * cols // 2 + 4, 1, chan), jnp.float32),
             pltpu.VMEM((2 * chan, 2 * hidden), jnp.bfloat16),
         ],
         compiler_params=pltpu.CompilerParams(

time: 8.7 us -> 8.7 us (level)
  no operation moved by 1% of the time
where the time goes in v5:
time: 8.7 us; the launch traced here: 8.55 us
  Pallas kernels  7.93 us (91%)
  local copies, waits for them, and re-layouts  0.61 us (7%)
    pallas_call x1, Pallas kernels, one_round(): pl.pallas_call(functools.partial(kernel, n_row), out_shape=pltpu.VMEM((ro...  7.93 us
    unnamed x1, local copies, waits for them, and re-layouts  0.61 us

profile of v5, /device:TPU:1, one launch (start us, length us, event | category | flops | bytes accessed | tf_op | source)
XLA Modules:
  0.0 8.5 jit_solution(8595103546837279645)
XLA Ops:
  0.0 7.9 %shard_map.109 = bf16[4,16,128]{2,1,0:T(8,128)(2,1)S(1)} custom-call(bf16[4,16,128]{2,1,0:T(8,128)(2,1)} %pair_hbm.1, f32[1,128]{1,0:T(1,128)} %bitcast.4, f32[1,128]{1,0:T(1,128)} %bitcast.5, bf16[128,128]{1,0:T(8,128)(2,1)} %wap_hbm.1, bf16[128,128]{1,0:T(8,128)(2,1)} %wag_hbm.1, bf16[128,128]{1,0:T(8,128)(2,1)} %wbp_hbm.1, bf16[128,128]{1,0:T(8,128)(2,1)} %wbg_hbm.1, ...), custom_call_target="tpu_custom_call" | custom-call | tf_op jit(solution)/shard_map/pallas_call | solution.py:434
  7.9 0.6 %copy.13 = bf16[4,16,128]{2,1,0:T(8,128)(2,1)} copy(bf16[4,16,128]{2,1,0:T(8,128)(2,1)S(1)} %shard_map.109) | data formatting | bytes 32768

commit v6 on v5

--- a/solution.py
+++ b/solution.py
@@ -372,31 +372,26 @@
         return far.astype(jnp.float32).reshape(2, rows, cols, hidden)
 
 
-    @pl.when(first)
-    def _():
-        arrived(0, 2 * split + 1)
-        for source in range(split):
+    for group in range(2):
+        own = jnp.logical_and(near, slot // split == group)
+
+        @pl.when(own)
+        def _():
+            arrived(group, 2 * split - group)
+
+        @pl.when(jnp.logical_not(own))
+        def _():
+            arrived(group, 2 * split + 1 - group)
+
+        if group == 1:
+
+            @pl.when(first)
+            def _():
+                far = project(half - 1).astype(jnp.bfloat16)
+                right_buf[2 * half - 2 :] = far
+
+        for source in range(group * split, (group + 1) * split):
             absorb(source, block_of(source))
-        arrived(1, 2 * split)
-        absorb(half - 1, project(half - 1))
-        for source in range(split, half - 1):
-            absorb(source, block_of(source))
-
-    @pl.when(jnp.logical_not(first))
-    def _():
-        for group in range(2):
-            own = jnp.logical_and(near, slot // split == group)
-
-            @pl.when(own)
-            def _():
-                arrived(group, 2 * split - group)
-
-            @pl.when(jnp.logical_not(own))
-            def _():
-                arrived(group, 2 * split + 1 - group)
-
-            for source in range(group * split, (group + 1) * split):
-                absorb(source, block_of(source))
 
     tri = tri_v[...].reshape(rows * cols, hidden).astype(jnp.bfloat16).astype(jnp.float32)
     tri_centred, tri_scale = centre(tri, vec_v[2])

time: 8.7 us -> 8.71 us (level)
  no operation moved by 1% of the time
where the time goes in v6:
time: 8.71 us; the launch traced here: 8.56 us
  Pallas kernels  7.94 us (91%)
  local copies, waits for them, and re-layouts  0.61 us (7%)
    pallas_call x1, Pallas kernels, one_round(): pl.pallas_call(functools.partial(kernel, n_row), out_shape=pltpu.VMEM((ro...  7.94 us
    unnamed x1, local copies, waits for them, and re-layouts  0.61 us

profile of v6, /device:TPU:1, one launch (start us, length us, event | category | flops | bytes accessed | tf_op | source)
XLA Modules:
  0.0 8.6 jit_solution(47264846432196312)
XLA Ops:
  0.0 7.9 %shard_map.109 = bf16[4,16,128]{2,1,0:T(8,128)(2,1)S(1)} custom-call(bf16[4,16,128]{2,1,0:T(8,128)(2,1)} %pair_hbm.1, f32[1,128]{1,0:T(1,128)} %bitcast.4, f32[1,128]{1,0:T(1,128)} %bitcast.5, bf16[128,128]{1,0:T(8,128)(2,1)} %wap_hbm.1, bf16[128,128]{1,0:T(8,128)(2,1)} %wag_hbm.1, bf16[128,128]{1,0:T(8,128)(2,1)} %wbp_hbm.1, bf16[128,128]{1,0:T(8,128)(2,1)} %wbg_hbm.1, ...), custom_call_target="tpu_custom_call" | custom-call | tf_op jit(solution)/shard_map/pallas_call | solution.py:429
  8.0 0.6 %copy.13 = bf16[4,16,128]{2,1,0:T(8,128)(2,1)} copy(bf16[4,16,128]{2,1,0:T(8,128)(2,1)S(1)} %shard_map.109) | data formatting | bytes 32768

commit v7 on v6

--- a/solution.py
+++ b/solution.py
@@ -390,8 +390,13 @@
                 far = project(half - 1).astype(jnp.bfloat16)
                 right_buf[2 * half - 2 :] = far
 
-        for source in range(group * split, (group + 1) * split):
-            absorb(source, block_of(source))
+        whole = right_buf[2 * group * split : 2 * (group + 1) * split].astype(jnp.float32)
+        whole = whole.reshape(split, 2, rows, cols // 8, 8, hidden)
+        for i in range(rows):
+            mine = left_buf[:, i].astype(jnp.float32).reshape(1, 2, 1, cols // 8, 8, hidden)
+            prod = jnp.sum(jnp.sum(mine * whole, axis=3), axis=1)
+            prod = jnp.sum(prod, axis=2).reshape(split * rows, hidden)
+            tri_v[i, group * split * rows : (group + 1) * split * rows, :] = prod
 
     tri = tri_v[...].reshape(rows * cols, hidden).astype(jnp.bfloat16).astype(jnp.float32)
     tri_centred, tri_scale = centre(tri, vec_v[2])

time: 8.71 us -> 8.71 us (level)
  no operation moved by 1% of the time
where the time goes in v7:
time: 8.71 us; the launch traced here: 8.55 us
  Pallas kernels  7.93 us (91%)
  local copies, waits for them, and re-layouts  0.61 us (7%)
    pallas_call x1, Pallas kernels, one_round(): pl.pallas_call(functools.partial(kernel, n_row), out_shape=pltpu.VMEM((ro...  7.93 us
    unnamed x1, local copies, waits for them, and re-layouts  0.61 us

profile of v7, /device:TPU:1, one launch (start us, length us, event | category | flops | bytes accessed | tf_op | source)
XLA Modules:
  0.0 8.6 jit_solution(6454114687013031668)
XLA Ops:
  0.0 7.9 %shard_map.109 = bf16[4,16,128]{2,1,0:T(8,128)(2,1)S(1)} custom-call(bf16[4,16,128]{2,1,0:T(8,128)(2,1)} %pair_hbm.1, f32[1,128]{1,0:T(1,128)} %bitcast.4, f32[1,128]{1,0:T(1,128)} %bitcast.5, bf16[128,128]{1,0:T(8,128)(2,1)} %wap_hbm.1, bf16[128,128]{1,0:T(8,128)(2,1)} %wag_hbm.1, bf16[128,128]{1,0:T(8,128)(2,1)} %wbp_hbm.1, bf16[128,128]{1,0:T(8,128)(2,1)} %wbg_hbm.1, ...), custom_call_target="tpu_custom_call" | custom-call | tf_op jit(solution)/shard_map/pallas_call | solution.py:434
  7.9 0.6 %copy.13 = bf16[4,16,128]{2,1,0:T(8,128)(2,1)} copy(bf16[4,16,128]{2,1,0:T(8,128)(2,1)S(1)} %shard_map.109) | data formatting | bytes 32768

commit v8 on v6

--- a/solution.py
+++ b/solution.py
@@ -146,7 +146,7 @@
         loads.append(pltpu.make_async_copy(vector, vec_v.at[n], in_sem.at[0]))
     for n, weight in enumerate(weights):
         span = w_v.at[:, n * hidden : (n + 1) * hidden]
-        loads.append(pltpu.make_async_copy(weight, span, in_sem.at[1 if n < 2 else 2]))
+        loads.append(pltpu.make_async_copy(weight, span, in_sem.at[1]))
 
     def loaded(span, index):
         pltpu.make_async_copy(span, span, in_sem.at[index]).wait()
@@ -247,7 +247,7 @@
     loaded(bytes_v, 0)
     pair = pair_v[...].astype(jnp.float32).reshape(rows * cols, chan)
     centred, scale = centre(pair, vec_v[0])
-    loaded(w_v.at[:, 0 : 2 * hidden], 1)
+    loaded(w_v, 1)
     right_shift = through(vec_v[1], w_v[:, 0 : 2 * hidden])
     right = gated(centred, scale, right_shift, w_v[:, 0 : 2 * hidden])
     right = right.reshape(rows, cols, hidden)
@@ -279,7 +279,6 @@
     def _():
         right_buf[2 * slot + sub] = right
 
-    loaded(w_v.at[:, 2 * hidden :], 2)
     left_shift = through(vec_v[1], w_v[:, 2 * hidden : 4 * hidden])
     left = gated(centred, scale, left_shift, w_v[:, 2 * hidden : 4 * hidden])
     left_buf[sub] = left.reshape(rows, cols, hidden)
@@ -439,7 +438,7 @@
             pltpu.VMEM((2 * half, rows, cols, hidden), jnp.bfloat16),
             pltpu.VMEM((2, rows, cols, hidden), jnp.bfloat16),
             pltpu.VMEM((rows, cols, hidden), jnp.float32),
-            pltpu.SemaphoreType.DMA((3,)),
+            pltpu.SemaphoreType.DMA((2,)),
             pltpu.SemaphoreType.DMA,
             pltpu.SemaphoreType.DMA((2,)),
             pltpu.SemaphoreType.REGULAR,

time: 8.71 us -> 8.73 us (level)
  no operation moved by 1% of the time
where the time goes in v8:
time: 8.73 us; the launch traced here: 8.58 us
  Pallas kernels  7.96 us (91%)
  local copies, waits for them, and re-layouts  0.61 us (7%)
    pallas_call x1, Pallas kernels, one_round(): pl.pallas_call(functools.partial(kernel, n_row), out_shape=pltpu.VMEM((ro...  7.96 us
    unnamed x1, local copies, waits for them, and re-layouts  0.61 us

profile of v8, /device:TPU:1, one launch (start us, length us, event | category | flops | bytes accessed | tf_op | source)
XLA Modules:
  0.0 8.6 jit_solution(10723567438939138420)
XLA Ops:
  0.0 8.0 %shard_map.109 = bf16[4,16,128]{2,1,0:T(8,128)(2,1)S(1)} custom-call(bf16[4,16,128]{2,1,0:T(8,128)(2,1)} %pair_hbm.1, f32[1,128]{1,0:T(1,128)} %bitcast.4, f32[1,128]{1,0:T(1,128)} %bitcast.5, bf16[128,128]{1,0:T(8,128)(2,1)} %wap_hbm.1, bf16[128,128]{1,0:T(8,128)(2,1)} %wag_hbm.1, bf16[128,128]{1,0:T(8,128)(2,1)} %wbp_hbm.1, bf16[128,128]{1,0:T(8,128)(2,1)} %wbg_hbm.1, ...), custom_call_target="tpu_custom_call" | custom-call | tf_op jit(solution)/shard_map/pallas_call | solution.py:428
  8.0 0.6 %copy.13 = bf16[4,16,128]{2,1,0:T(8,128)(2,1)} copy(bf16[4,16,128]{2,1,0:T(8,128)(2,1)S(1)} %shard_map.109) | data formatting | bytes 32768
